TPU v7x, 256 devices: a whole 4x4x8 slice. The times are simulated.
256 devices in a mesh: feat: 128 (over z, x, y), rep: 2 (over core).
Axes of the slice: x: 4, y: 4, z: 8, core: 2. Of those that a mesh axis runs over, the one named last changes fastest.
Arguments:
- inputs: bfloat16 [1024, 440], P('rep'), may hold values from -6 to 6
- targets: bfloat16 [1024, 512], P('rep'), may hold values from -6 to 6
- frequencies: bfloat16 [440, 524288], P(None, ('feat', 'rep')), may hold values from -1.5 to 1.5
- phases: float32 [524288], P(('feat', 'rep')), may hold values from 0 to 6.2832
- weights: bfloat16 [524288, 512], P(('feat', 'rep')), may hold values from -6 to 6
- eigvecs: bfloat16 [524288, 256], P(('feat', 'rep')), may hold values from -0.125 to 0.125
- eigvals: float32 [256], replicated, may hold values from 0.1 to 1
- tail: float32 [1], replicated, may hold values from 0.02 to 0.08
Outputs:
- new_weights: bfloat16 [524288, 512], P(('feat', 'rep'))
- residual: float32 [1024, 512], P(None, ('feat', 'rep'))
All inputs are finite; a program needn't handle non-finite values.
Results may differ from a plain program's by a relative error of at most 0.0045.
Values may be sent and summed in bfloat16 or wider, within the bound.
A program may use at most 64 MiB of HBM per device.

v0:
```python
import math

import jax
import jax.numpy as jnp
from jax import lax
from jax.sharding import PartitionSpec as P


def split_parts(values):
    upper = values.astype(jnp.bfloat16)
    upper_back = lax.optimization_barrier(upper).astype(jnp.float32)
    lower = (values - upper_back).astype(jnp.bfloat16)
    return (upper, lower)


def mixed_product(left_bf, right_f32, dims):
    upper, lower = split_parts(right_f32)
    first = lax.dot_general(left_bf, upper, dims, preferred_element_type=jnp.float32)
    second = lax.dot_general(left_bf, lower, dims, preferred_element_type=jnp.float32)
    return first + second


def shards(inputs, targets, frequencies, phases, weights, eigvecs, eigvals, tail):
    rows_in, rows_tgt = (
        lax.all_gather(inputs, "rep", axis=0, tiled=True),
        lax.all_gather(targets, "rep", axis=0, tiled=True),
    )
    devices_all = lax.axis_size("feat") * lax.axis_size("rep")
    total_feats = weights.shape[0] * devices_all
    theta = jnp.dot(rows_in, frequencies, preferred_element_type=jnp.float32) + phases[None, :]
    feats = (math.sqrt(2.0 / total_feats) * jnp.cos(theta)).astype(jnp.bfloat16)
    partial_value = jnp.dot(feats, weights, preferred_element_type=jnp.float32)
    width_cols = weights.shape[1] // devices_all
    start = lax.axis_index(("feat", "rep")) * width_cols
    pred = lax.psum(partial_value, ("feat", "rep"))
    full_resid = pred - rows_tgt.astype(jnp.float32)
    resid_b = full_resid.astype(jnp.bfloat16)
    residual = lax.dynamic_slice_in_dim(full_resid, start, width_cols, 1)
    grad = lax.dot_general(
        feats, resid_b, (((0,), (0,)), ((), ())), preferred_element_type=jnp.float32
    )
    local_coeff = mixed_product(eigvecs, grad, (((0,), (0,)), ((), ())))
    coeff = lax.psum(local_coeff, ("feat", "rep"))
    damp = 1.0 - tail[0] / eigvals
    correction = mixed_product(eigvecs, damp[:, None] * coeff, (((1,), (0,)), ((), ())))
    new_weights = weights.astype(jnp.float32) - (grad - correction) / tail[0]
    return (new_weights.astype(jnp.bfloat16), residual)


def solution(mesh):
    in_specs = (
        P("rep", None),
        P("rep", None),
        P(None, ("feat", "rep")),
        P(("feat", "rep")),
        P(("feat", "rep"), None),
        P(("feat", "rep"), None),
        P(),
        P(),
    )
    out_specs = (P(("feat", "rep"), None), P(None, ("feat", "rep")))
    return jax.shard_map(shards, mesh=mesh, in_specs=in_specs, out_specs=out_specs, check_vma=False)
```

profile of v0, /device:TPU:1, one launch (start us, length us, event | category | flops | bytes accessed | tf_op | source)
XLA Modules:
  0.0 588.3 jit_solution(2445106770315207424)
XLA Ops:
  8.0 0.0 copy-start
  8.0 0.0 all-reduce.3.cloned.1.call-start
  8.1 5.7 all_gather.6
  13.7 0.0 copy-done
  13.7 0.0 copy-start.7
  13.7 33.2 %multiply_convert_fusion = bf16[1024,2048]{1,0:T(8,128)(2,1)S(1)} fusion(f32[2048]{0:T(1024)} %param.11, bf16[1024,440]{0,1:T(8,128)(2,1)S(1)} %all_gather.6, bf16[440,2048]{1,0:T(8,128)(2,1)S(1)} %copy-done), kind=kOutput, calls=%fused_computation | convolution fusion | flops 1851785216 | bytes 6905856 | tf_op jit(solution)/shard_map/dot_general | solution.py:30
  46.9 0.0 copy-start.8
  46.9 1.9 copy-done.8
  48.9 0.0 copy-done.7
  48.9 3.6 fusion.9
  52.5 0.0 all-reduce.3.cloned.1.call-update
  52.5 0.0 all-gather.2.cloned.1.call-start
  52.6 0.5 all-gather.2.cloned.1.call-update
  53.1 0.0 all-reduce.5.cloned.1.call-start
  53.8 259.5 %all-reduce.3.cloned.1.call-done = f32[1024,512]{1,0:T(8,128)} async-done(((f32[1024,512]{1,0:T(8,128)}), f32[1024,512]{1,0:T(8,128)}) %all-reduce.3.cloned.1.call-update) | async-done | bytes 2097168 | tf_op jit(solution)/shard_map/psum | solution.py:35
  313.4 0.0 all-gather.2.cloned.1.call-done
  313.4 0.0 copy-start.9
  313.4 2.3 convert_subtract_fusion
  315.7 0.8 copy-done.9
  316.5 0.0 copy-start.4
  316.5 0.0 copy-start.1
  316.5 2.4 fusion.8
  318.9 0.0 copy-done.4
  318.9 0.0 copy-start.2
  318.9 1.9 copy-done.2
  320.9 0.0 copy-done.1
  320.9 1.0 fusion.3
  321.9 0.0 copy-start.6
  321.9 1.5 fusion.4
  323.4 0.0 all-reduce.5.cloned.1.call-update
  323.5 0.0 copy-done.6
  323.5 1.2 constant_dynamic-slice_fusion
  324.7 0.8 copy.12
  325.5 248.8 %all-reduce.5.cloned.1.call-done = f32[256,512]{0,1:T(8,128)} async-done(((f32[256,512]{0,1:T(8,128)}), f32[256,512]{0,1:T(8,128)}) %all-reduce.5.cloned.1.call-update) | async-done | bytes 524304 | tf_op jit(solution)/shard_map/psum | solution.py:43
  574.3 0.0 copy-start.3
  574.3 0.0 copy-start.5
  574.3 1.2 multiply_convert_fusion.1
  575.6 0.7 fusion.10
  576.3 0.4 copy-done.3
  576.7 0.1 copy-done.5
  576.8 4.1 fusion.2
  (1 shorter events, 0.0 us)
Async XLA Ops:
  8.0 5.7 copy-start
  8.0 305.3 %all-reduce.3.cloned.1.call-start = ((), (), s32[]{:S(2)}) async-start(), calls=%async_computation | async-start | bytes 4194304 | tf_op jit(solution)/shard_map/psum | solution.py:35
  13.7 35.2 %copy-start.7 = (bf16[2048,512]{1,0:T(8,128)(2,1)S(1)}, bf16[2048,512]{1,0:T(8,128)(2,1)}, u32[]{:S(2)}) copy-start(bf16[2048,512]{1,0:T(8,128)(2,1)} %param.12) | copy-start | bytes 6291460
  46.9 1.9 copy-start.8
  52.5 260.8 %all-gather.2.cloned.1.call-start = ((), (), s32[]{:S(2)}) async-start(), calls=%async_computation.1 | async-start | bytes 1572864 | tf_op jit(solution)/shard_map/all_gather | solution.py:26
  53.1 521.2 %all-reduce.5.cloned.1.call-start = ((), (), s32[]{:S(2)}) async-start(), calls=%async_computation.2 | async-start | bytes 1048576 | tf_op jit(solution)/shard_map/psum | solution.py:43
  313.4 3.1 copy-start.9
  316.5 2.4 copy-start.4
  316.5 4.4 copy-start.1
  318.9 1.9 copy-start.2
  321.9 1.6 copy-start.6
  574.3 2.3 copy-start.3
  574.3 2.5 copy-start.5
Sparse Core Ops, SparseCore 0:
  52.7 260.6 all-reduce.2
  323.6 250.7 all-reduce.4
Sparse Core Ops, SparseCore 1:
  54.8 15.9 all-gather.1
where the time goes:
time: 589 us; the launch traced here: 588 us
  waiting for transfers between devices  509 us (86%)
  matrix products  46.6 us (8%)
  between operations  16.2 us (3%)
  local copies, waits for them, and re-layouts  7.2 us (1%)
    psum x1, waiting for transfers between devices, shards(): pred = lax.psum(partial_value, ('feat', 'rep'))  260 us
    psum x1, waiting for transfers between devices, shards(): coeff = lax.psum(local_coeff, ('feat', 'rep'))  249 us
    dot_general x1, matrix products, shards(): jnp.dot(rows_in, frequencies, preferred_element_type=jnp.float32)  33.2 us
  transfers between devices with their start and end apart: 3, of which 2 were waited for; matrix products, arithmetic and copies ran while one was open for 0% of the time, Pallas kernels for 0%

commit v1 on v0

v1 whole, which is shorter than its diff:
```python
import functools
import math

import jax
import jax.numpy as jnp
from jax import lax
from jax.experimental import pallas as pl
from jax.experimental.pallas import tpu as pltpu
from jax.sharding import PartitionSpec as P

MESH = pl.DeviceIdType.MESH
BF, F32 = jnp.bfloat16, jnp.float32
FEATURES = 524288
SCALE = math.sqrt(2.0 / FEATURES)
INV_TURN = 1.0 / (2.0 * math.pi)
SIN = (6.283164044300404, -41.33714237083565, 81.34076887918835, -70.99343319450264)
NP = 4


def scaled_cos(theta, turns):
    t = theta * INV_TURN + turns
    s = 0.25 - jnp.abs(t - jnp.round(t))
    u = s * s
    p = SIN[3] * SCALE
    for q in SIN[2::-1]:
        p = p * u + q * SCALE
    return (s * p).astype(BF)


def kernel(
    in_hbm, targ_hbm, freq_hbm, w_hbm, e_hbm, phase_ref, eig_ref, tail_ref,
    out_hbm, res_hbm,
    x_v, freq_v, we_v, targ_v, scale_v, feat_v, ft_v, g_v,
    own_v, send_c, recv_c, buf_a, recv_a, own_b, buf_b, recv_b, recv_z,
    gath, rk_v, out_v, res_v,
    load_sem, store_sem, sx, rx, sc, rc, sa, ra, sb, rb, sz, rz, sgb, rgb, sga, rga, sgc, rgc,
):
    f, c = lax.axis_index("feat"), lax.axis_index("rep")
    z, x, y = f // 16, (f // 4) % 4, f % 4

    def at_x(d):
        return (z * 16 + ((x + d) % 4) * 4 + y, c)

    def at_y(d):
        return (z * 16 + x * 4 + (y + d) % 4, c)

    def at_z(d):
        return (((z + d) % 8) * 16 + x * 4 + y, c)

    mate = (f, 1 - c)
    barrier = pltpu.get_barrier_semaphore()
    everyone = [mate]
    everyone += [at_x(d) for d in (1, 2, 3)] + [at_y(d) for d in (1, 2, 3)]
    everyone += [at_z(d) for d in range(1, 8)]
    for peer in everyone:
        pl.semaphore_signal(barrier, inc=1, device_id=peer, device_id_type=MESH)

    loads = [
        (in_hbm, x_v.at[0]),
        (freq_hbm, freq_v),
        (w_hbm, we_v.at[:, 0:512]),
        (e_hbm, we_v.at[:, 512:768]),
        (targ_hbm.at[:, 0:384], targ_v.at[0]),
        (targ_hbm.at[:, 384:512], targ_v.at[1, :, 0:128]),
    ]
    loads = [pltpu.make_async_copy(s, d, load_sem.at[i]) for i, (s, d) in enumerate(loads)]
    for load in loads:
        load.start()
    targ_v[1, :, 128:384] = jnp.zeros((512, 256), BF)
    scale_v[...] = jnp.ones_like(scale_v)
    scale_v[1, :, 128:384] = 1.0 - tail_ref[...] / eig_ref[...]

    def remote(src, dst, send, recv, peer):
        return pltpu.make_async_remote_copy(
            src_ref=src, dst_ref=dst, send_sem=send, recv_sem=recv,
            device_id=peer, device_id_type=MESH,
        )

    def first(p):
        return (x, at_x) if p % 2 == 0 else (y, at_y)

    def second(p):
        return (y, at_y) if p % 2 == 0 else (x, at_x)

    def core_copy(p):
        return remote(send_c.at[p], recv_c.at[p], sc.at[p], rc.at[p], mate)

    def a_copies(p):
        i, peer = first(p)
        return [
            remote(buf_a.at[p, pl.ds(((i + d) % 4) * 4, 4)], recv_a.at[p, d - 1], sa.at[p, d - 1], ra.at[p, d - 1], peer(d))
            for d in (1, 2, 3)
        ]

    def b_copies(p):
        i, peer = second(p)
        return [
            remote(buf_b.at[p, (i + d) % 4], recv_b.at[p, d - 1], sb.at[p, d - 1], rb.at[p, d - 1], peer(d))
            for d in (1, 2, 3)
        ]

    def z_copies(p):
        return [
            remote(recv_z.at[p, z], recv_z.at[p, z], sz.at[p, d - 1], rz.at[p, d - 1], at_z(d))
            for d in range(1, 8)
        ]

    def gb_copies(p):
        i, (k, peer) = first(p)[0], second(p)
        here = gath.at[p, 0, i * 4 + k]
        return [remote(here, here, sgb.at[p, d - 1], rgb.at[p, d - 1], peer(d)) for d in (1, 2, 3)]

    def ga_copies(p):
        i, peer = first(p)
        here = gath.at[p, 0, pl.ds(i * 4, 4)]
        return [remote(here, here, sga.at[p, d - 1], rga.at[p, d - 1], peer(d)) for d in (1, 2, 3)]

    def gc_copy(p):
        return remote(gath.at[p, 0], gath.at[p, 1], sgc.at[p], rgc.at[p], mate)

    def start(copies):
        for copy in copies:
            copy.start()

    def arrived(copies):
        for copy in copies:
            copy.wait_recv()

    def sent(copies):
        for copy in copies:
            copy.wait_send()

    turns = phase_ref[...] * INV_TURN

    def features(half, pair):
        def tile(n, carry):
            cols = pl.ds(pl.multiple_of(n * 1024, 1024), 1024)
            theta = jnp.dot(x_v[half, pl.ds(pair * 256, 256), :], freq_v[:, cols], preferred_element_type=F32)
            value = scaled_cos(theta, phase_ref[:, cols] * INV_TURN)
            for q in (0, 1):
                feat_v[2 * pair + q, pl.ds(half * 128, 128), cols] = value[q * 128:(q + 1) * 128]
            return carry

        lax.fori_loop(0, 2, tile, 0)

    def project(p):
        def tile(n, carry):
            cols = pl.ds(pl.multiple_of(n * 256, 256), 256)
            part = jnp.dot(feat_v[p], we_v[:, cols], preferred_element_type=F32)
            own_v[p, :, cols] = part[0:128]
            send_c[p, :, cols] = part[128:256].astype(BF)
            return carry

        lax.fori_loop(0, 3, tile, 0)
        core_copy(p).start()

    def stage_1(p):
        arrived([core_copy(p)])
        for i in range(4):
            for j in range(2):
                rows = pl.ds(32 * i + 16 * j, 16)
                total = own_v[p, rows, :] + recv_c[p, rows, :].astype(F32)
                own_v[p, rows, :] = total
                for k in range(2):
                    buf_a[p, 4 * i + 2 * j + k] = total[:, 384 * k:384 * (k + 1)].astype(BF)
        start(a_copies(p))
        sent([core_copy(p)])

    def stage_2(p):
        arrived(a_copies(p))
        i = first(p)[0]
        for j in range(2):
            rows = pl.ds(pl.multiple_of(32 * i + 16 * j, 16), 16)
            for k in range(2):
                b = 2 * j + k
                total = own_v[p, rows, 384 * k:384 * (k + 1)]
                for d in range(3):
                    total = total + recv_a[p, d, b].astype(F32)
                own_b[p, b] = total
                buf_b[p, b] = total.astype(BF)
        start(b_copies(p))
        sent(a_copies(p))

    def stage_3(p):
        arrived(b_copies(p))
        k = second(p)[0]
        total = own_b[p, k]
        for d in range(3):
            total = total + recv_b[p, d].astype(F32)
        recv_z[p, z] = total.astype(BF)
        start(z_copies(p))
        sent(b_copies(p))

    def stage_4(p):
        arrived(z_copies(p))
        i, k = first(p)[0], second(p)[0]
        total = recv_z[p, 0].astype(F32)
        for d in range(1, 8):
            total = total + recv_z[p, d].astype(F32)
        rows = pl.ds(pl.multiple_of(p * 128 + 32 * i + 16 * (k // 2), 16), 16)
        total = total * scale_v[k % 2] - targ_v[k % 2, rows, :].astype(F32)
        gath[p, 0, i * 4 + k] = total.astype(BF)
        start(gb_copies(p))
        sent(z_copies(p))

    def stage_5(p):
        arrived(gb_copies(p))
        start(ga_copies(p))
        sent(gb_copies(p))

    def stage_6(p):
        arrived(ga_copies(p))
        gc_copy(p).start()
        sent(ga_copies(p))

    column = 4 * f + 2 * c

    def stage_7(p):
        arrived([gc_copy(p)])
        for half in range(2):
            for b in range(16):
                rows = half * 128 + 32 * (b // 4) + 16 * ((b % 4) // 2)
                rk_v[p, rows:rows + 16, 384 * (b % 2):384 * (b % 2 + 1)] = gath[p, half, b]
        sent([gc_copy(p)])
        pick = lax.broadcasted_iota(jnp.int32, (8, 512), 1) == lax.broadcasted_iota(jnp.int32, (8, 512), 0) + column
        pick = jnp.where(pick, 1.0, 0.0).astype(BF)
        shown = lax.dot_general(pick, rk_v[p, :, 0:512], (((1,), (1,)), ((), ())), preferred_element_type=F32)
        for half in range(2):
            res_v[half, :, p * 128:(p + 1) * 128] = shown[:, half * 128:(half + 1) * 128]
        resid = rk_v[p, :, 0:512]
        coeff = lax.dot_general(
            rk_v[p, :, 512:768], resid, (((0,), (0,)), ((), ())), preferred_element_type=F32
        )
        coeff = (-coeff).astype(BF)
        last = p == NP - 1
        rate = 1.0 / tail_ref[...]

        def tile(n, carry):
            rows = pl.ds(pl.multiple_of(n * 512, 512), 512)
            part = jnp.dot(ft_v[p, rows, :], resid, preferred_element_type=F32)
            part = part + jnp.dot(we_v[rows, 512:768], coeff, preferred_element_type=F32)
            if p > 0:
                part = part + g_v[rows, :]
            if last:
                out_v[rows, :] = (we_v[rows, 0:512].astype(F32) - part * rate).astype(BF)
                pltpu.make_async_copy(out_v.at[rows], out_hbm.at[rows], store_sem.at[n]).start()
            else:
                g_v[rows, :] = part
            return carry

        lax.fori_loop(0, 4, tile, 0)

    def flip(p):
        def tile(n, carry):
            cols = pl.ds(pl.multiple_of(n * 256, 256), 256)
            ft_v[p, cols, :] = feat_v[p, :, cols].T
            return carry

        lax.fori_loop(0, 8, tile, 0)

    loads[0].wait()
    loads[1].wait()
    features(0, 0)
    pl.semaphore_wait(barrier, len(everyone))
    trade = remote(in_hbm, x_v.at[1], sx, rx, mate)
    trade.start()
    features(0, 1)
    for load in loads[2:]:
        load.wait()
    trade.wait()
    features(1, 0)
    project(0)
    project(1)
    stage_1(0)
    features(1, 1)
    stage_1(1)
    project(2)
    project(3)
    stage_1(2)
    stage_2(0)
    stage_1(3)
    flip(0)
    stage_2(1)
    flip(1)
    stage_3(0)
    stage_2(2)
    flip(2)
    stage_3(1)
    stage_2(3)
    flip(3)
    stage_4(0)
    stage_3(2)
    stage_4(1)
    stage_3(3)
    stage_5(0)
    stage_4(2)
    stage_5(1)
    stage_4(3)
    stage_6(0)
    stage_5(2)
    stage_6(1)
    stage_5(3)
    stage_7(0)
    stage_6(2)
    stage_7(1)
    stage_6(3)
    stage_7(2)
    stage_7(3)
    shown = [
        pltpu.make_async_copy(res_v.at[0], res_hbm.at[c], store_sem.at[4]),
        pltpu.make_async_copy(res_v.at[1], res_hbm.at[1 - c], store_sem.at[5]),
    ]
    start(shown)
    for n in range(4):
        rows = pl.ds(n * 512, 512)
        pltpu.make_async_copy(out_v.at[rows], out_hbm.at[rows], store_sem.at[n]).wait()
    for copy in shown:
        copy.wait()


def shards(inputs, targets, frequencies, phases, weights, eigvecs, eigvals, tail):
    hbm = pl.BlockSpec(memory_space=pl.ANY)
    vmem = pl.BlockSpec(memory_space=pltpu.VMEM)
    dma = pltpu.SemaphoreType.DMA
    chunk = (16, 384)
    new_weights, shown = pl.pallas_call(
        kernel,
        out_shape=[
            jax.ShapeDtypeStruct((2048, 512), BF),
            jax.ShapeDtypeStruct((2, 8, 512), F32),
        ],
        in_specs=[hbm] * 5 + [vmem] * 3,
        out_specs=[hbm, hbm],
        scratch_shapes=[
            pltpu.VMEM((2, 512, 440), BF),
            pltpu.VMEM((440, 2048), BF),
            pltpu.VMEM((2048, 768), BF),
            pltpu.VMEM((2, 512, 384), BF),
            pltpu.VMEM((2, 1, 384), F32),
            pltpu.VMEM((NP, 256, 2048), BF),
            pltpu.VMEM((NP, 2048, 256), BF),
            pltpu.VMEM((2048, 512), F32),
            pltpu.VMEM((NP, 128, 768), F32),
            pltpu.VMEM((NP, 128, 768), BF),
            pltpu.VMEM((NP, 128, 768), BF),
            pltpu.VMEM((NP, 16) + chunk, BF),
            pltpu.VMEM((NP, 3, 4) + chunk, BF),
            pltpu.VMEM((NP, 4) + chunk, F32),
            pltpu.VMEM((NP, 4) + chunk, BF),
            pltpu.VMEM((NP, 3) + chunk, BF),
            pltpu.VMEM((NP, 8) + chunk, BF),
            pltpu.VMEM((NP, 2, 16) + chunk, BF),
            pltpu.VMEM((NP, 256, 768), BF),
            pltpu.VMEM((2048, 512), BF),
            pltpu.VMEM((2, 8, 512), F32),
            dma((6,)), dma((6,)),
            dma, dma,
            dma((NP,)), dma((NP,)),
            dma((NP, 3)), dma((NP, 3)),
            dma((NP, 3)), dma((NP, 3)),
            dma((NP, 7)), dma((NP, 7)),
            dma((NP, 3)), dma((NP, 3)),
            dma((NP, 3)), dma((NP, 3)),
            dma((NP,)), dma((NP,)),
        ],
        compiler_params=pltpu.CompilerParams(
            collective_id=0, has_side_effects=True, vmem_limit_bytes=60 << 20
        ),
        name="step",
    )(
        inputs, targets, frequencies, weights, eigvecs,
        phases.reshape(1, -1), eigvals.reshape(1, -1), tail.reshape(1, 1),
    )
    residual = shown[:, 0:2, :].transpose(0, 2, 1).reshape(1024, 2)
    return (new_weights, residual)


def solution(mesh):
    in_specs = (
        P("rep", None),
        P("rep", None),
        P(None, ("feat", "rep")),
        P(("feat", "rep")),
        P(("feat", "rep"), None),
        P(("feat", "rep"), None),
        P(),
        P(),
    )
    out_specs = (P(("feat", "rep"), None), P(None, ("feat", "rep")))
    return jax.shard_map(shards, mesh=mesh, in_specs=in_specs, out_specs=out_specs, check_vma=False)
```

time: 589 us -> 61.2 us (0.10)
  waiting for transfers between devices: 509 us -> 0 us
  Pallas kernels: 0 us -> 53.3 us
  matrix products: 46.6 us -> 0 us
  between operations: 16.2 us -> 1.29 us
    psum x2 -> x0, waiting for transfers between devices: 508 us -> none  [the longest x1 260 us: shards(): pred = lax.psum(partial_value, ('feat', 'rep'))]
    pallas_call x0 -> x1, Pallas kernels: none -> 53.3 us  [shards(): pl.pallas_call(kernel, out_shape=[jax.ShapeDtypeStruct((2048, 512), BF),...]
    dot_general x7 -> x0, matrix products: 46.6 us -> none  [the longest x1 33.2 us: shards(): jnp.dot(rows_in, frequencies, preferred_element_type=jnp.float32)]
  transfers between devices with their start and end apart: 3 -> 0, of which waited for: 2 -> 0; matrix products, arithmetic and copies ran while one was open for 0% -> 0% of each run, Pallas kernels for 0% -> 0%
where the time goes in v1:
time: 61.2 us; the launch traced here: 61 us
  Pallas kernels  53.3 us (87%)
  local copies, waits for them, and re-layouts  6.42 us (10%)
  between operations  1.29 us (2%)
    pallas_call x1, Pallas kernels, shards(): pl.pallas_call(kernel, out_shape=[jax.ShapeDtypeStruct((2048, 512), BF),...  53.3 us
    unnamed x2, local copies, waits for them, and re-layouts  5.06 us
    slice x1, local copies, waits for them, and re-layouts, shards(): residual = shown[:, 0:2, :].transpose(0, 2, 1).reshape(1024, 2)  1.36 us

profile of v1, /device:TPU:1, one launch (start us, length us, event | category | flops | bytes accessed | tf_op | source)
XLA Modules:
  0.0 61.0 jit_solution(11360111367991055375)
XLA Ops:
  1.3 2.0 %copy.10.in_hbm = bf16[512,440]{1,0:T(8,128)(2,1)} copy(bf16[512,440]{0,1:T(8,128)(2,1)} %param.8) | data formatting | bytes 901120 | tf_op args[0]
  3.3 53.3 %step.1 = (bf16[2048,512]{1,0:T(8,128)(2,1)}, f32[2,8,512]{2,1,0:T(8,128)}) custom-call(bf16[512,440]{1,0:T(8,128)(2,1)} %copy.10.in_hbm, bf16[512,512]{1,0:T(8,128)(2,1)} %targ_hbm.1, bf16[440,2048]{1,0:T(8,128)(2,1)} %freq_hbm.1, bf16[2048,512]{1,0:T(8,128)(2,1)} %w_hbm.1, bf16[2048,256]{1,0:T(8,128)(2,1)} %e_hbm.1, f32[1,2048]{1,0:T(1,128)} %bitcast.7, ...), custom_call_target="tpu_custom_call" | custom-call | tf_op jit(solution)/shard_map/step/pallas_call | solution.py:326
  56.6 1.4 %slice.3 = f32[2,2,512]{2,1,0:T(2,128)} slice(f32[2,8,512]{2,1,0:T(8,128)} %get-tuple-element.5), slice={[0:2], [0:2], [0:512]} | slice | bytes 16384 | tf_op jit(solution)/shard_map/slice | solution.py:374
  57.9 3.0 %copy.13 = bf16[2048,512]{1,0:T(8,128)(2,1)} copy(bf16[2048,512]{1,0:T(8,128)(2,1)} %get-tuple-element.8) | data formatting | bytes 4194304

commit v2 on v1

--- a/solution.py
+++ b/solution.py
@@ -28,12 +28,12 @@
 
 
 def kernel(
-    in_hbm, targ_hbm, freq_hbm, w_hbm, e_hbm, phase_ref, eig_ref, tail_ref,
-    out_hbm, res_hbm,
-    x_v, freq_v, we_v, targ_v, scale_v, feat_v, ft_v, g_v,
+    order, in_hbm, targ_hbm, freq_hbm, w_hbm, e_hbm, phase_ref, eig_ref, tail_ref,
+    we_v, g_v, ft_last, resid_last, coeff_last, res_v,
+    x_v, freq_v, targ_v, scale_v, feat_v, ft_v,
     own_v, send_c, recv_c, buf_a, recv_a, own_b, buf_b, recv_b, recv_z,
-    gath, rk_v, out_v, res_v,
-    load_sem, store_sem, sx, rx, sc, rc, sa, ra, sb, rb, sz, rz, sgb, rgb, sga, rga, sgc, rgc,
+    gath, rk_v,
+    load_sem, sx, rx, sc, rc, sa, ra, sb, rb, sz, rz, sgb, rgb, sga, rga, sgc, rgc,
 ):
     f, c = lax.axis_index("feat"), lax.axis_index("rep")
     z, x, y = f // 16, (f // 4) % 4, f % 4
@@ -130,12 +130,13 @@
         for copy in copies:
             copy.wait_send()
 
-    turns = phase_ref[...] * INV_TURN
-
     def features(half, pair):
         def tile(n, carry):
             cols = pl.ds(pl.multiple_of(n * 1024, 1024), 1024)
-            theta = jnp.dot(x_v[half, pl.ds(pair * 256, 256), :], freq_v[:, cols], preferred_element_type=F32)
+            theta = lax.dot_general(
+                x_v[half, :, pl.ds(pair * 256, 256)], freq_v[:, cols], (((0,), (0,)), ((), ())),
+                preferred_element_type=F32,
+            )
             value = scaled_cos(theta, phase_ref[:, cols] * INV_TURN)
             for q in (0, 1):
                 feat_v[2 * pair + q, pl.ds(half * 128, 128), cols] = value[q * 128:(q + 1) * 128]
@@ -232,8 +233,10 @@
             rk_v[p, :, 512:768], resid, (((0,), (0,)), ((), ())), preferred_element_type=F32
         )
         coeff = (-coeff).astype(BF)
-        last = p == NP - 1
-        rate = 1.0 / tail_ref[...]
+        if p == NP - 1:
+            resid_last[...] = resid
+            coeff_last[...] = coeff
+            return
 
         def tile(n, carry):
             rows = pl.ds(pl.multiple_of(n * 512, 512), 512)
@@ -241,11 +244,7 @@
             part = part + jnp.dot(we_v[rows, 512:768], coeff, preferred_element_type=F32)
             if p > 0:
                 part = part + g_v[rows, :]
-            if last:
-                out_v[rows, :] = (we_v[rows, 0:512].astype(F32) - part * rate).astype(BF)
-                pltpu.make_async_copy(out_v.at[rows], out_hbm.at[rows], store_sem.at[n]).start()
-            else:
-                g_v[rows, :] = part
+            g_v[rows, :] = part
             return carry
 
         lax.fori_loop(0, 4, tile, 0)
@@ -253,69 +252,58 @@
     def flip(p):
         def tile(n, carry):
             cols = pl.ds(pl.multiple_of(n * 256, 256), 256)
-            ft_v[p, cols, :] = feat_v[p, :, cols].T
+            turned = feat_v[p, :, cols].T
+            if p == NP - 1:
+                ft_last[cols, :] = turned
+            else:
+                ft_v[p, cols, :] = turned
             return carry
 
         lax.fori_loop(0, 8, tile, 0)
 
-    loads[0].wait()
-    loads[1].wait()
-    features(0, 0)
-    pl.semaphore_wait(barrier, len(everyone))
     trade = remote(in_hbm, x_v.at[1], sx, rx, mate)
-    trade.start()
-    features(0, 1)
-    for load in loads[2:]:
-        load.wait()
-    trade.wait()
-    features(1, 0)
-    project(0)
-    project(1)
-    stage_1(0)
-    features(1, 1)
-    stage_1(1)
-    project(2)
-    project(3)
-    stage_1(2)
-    stage_2(0)
-    stage_1(3)
-    flip(0)
-    stage_2(1)
-    flip(1)
-    stage_3(0)
-    stage_2(2)
-    flip(2)
-    stage_3(1)
-    stage_2(3)
-    flip(3)
-    stage_4(0)
-    stage_3(2)
-    stage_4(1)
-    stage_3(3)
-    stage_5(0)
-    stage_4(2)
-    stage_5(1)
-    stage_4(3)
-    stage_6(0)
-    stage_5(2)
-    stage_6(1)
-    stage_5(3)
-    stage_7(0)
-    stage_6(2)
-    stage_7(1)
-    stage_6(3)
-    stage_7(2)
-    stage_7(3)
-    shown = [
-        pltpu.make_async_copy(res_v.at[0], res_hbm.at[c], store_sem.at[4]),
-        pltpu.make_async_copy(res_v.at[1], res_hbm.at[1 - c], store_sem.at[5]),
-    ]
-    start(shown)
+
+    def ready(n):
+        for load in (loads[0:2], loads[2:])[n]:
+            load.wait()
+
+    def greet(n):
+        pl.semaphore_wait(barrier, len(everyone))
+        trade.start()
+
+    steps = dict(
+        L=ready, B=greet, T=lambda n: trade.wait(), F=lambda n: features(0, n), M=lambda n: features(1, n), P=project,
+        X=flip, a=stage_1, b=stage_2, c=stage_3, d=stage_4, e=stage_5, f=stage_6, g=stage_7,
+    )
+    for op in " ".join(order).split():
+        steps[op[0]](int(op[1:]))
+
+
+def finish(we_v, g_v, ft_last, resid_last, coeff_last, shown_v, tail_ref, out_hbm, res_ref, out_v, store_sem):
+    rate = 1.0 / tail_ref[...]
+
+    def tile(n, carry):
+        rows = pl.ds(pl.multiple_of(n * 512, 512), 512)
+        part = jnp.dot(ft_last[rows, :], resid_last[...], preferred_element_type=F32)
+        part = part + jnp.dot(we_v[rows, 512:768], coeff_last[...], preferred_element_type=F32)
+        part = part + g_v[rows, :]
+        out_v[rows, :] = (we_v[rows, 0:512].astype(F32) - part * rate).astype(BF)
+        pltpu.make_async_copy(out_v.at[rows], out_hbm.at[rows], store_sem.at[n]).start()
+        return carry
+
+    lax.fori_loop(0, 4, tile, 0)
+    c = lax.axis_index("rep")
+    res_ref[:, pl.ds(pl.multiple_of(c * 512, 512), 512)] = shown_v[0, 0:2, :]
+    res_ref[:, pl.ds(pl.multiple_of((1 - c) * 512, 512), 512)] = shown_v[1, 0:2, :]
     for n in range(4):
         rows = pl.ds(n * 512, 512)
         pltpu.make_async_copy(out_v.at[rows], out_hbm.at[rows], store_sem.at[n]).wait()
-    for copy in shown:
-        copy.wait()
+
+
+ORDER = (
+    "L0 F0 B0 F1", "L1 T0 M0", "P0 P1 a0 M1", "a1 P2 P3 a2", "b0 a3 X0 b1", "X1 c0 b2 X2", "c1 b3 X3 d0",
+    "c2 d1 c3 e0", "d2 e1 d3 f0", "e2 f1 e3 g0", "f2 g1 f3 g2", "g3",
+)
 
 
 def shards(inputs, targets, frequencies, phases, weights, eigvecs, eigvals, tail):
@@ -323,23 +311,26 @@
     vmem = pl.BlockSpec(memory_space=pltpu.VMEM)
     dma = pltpu.SemaphoreType.DMA
     chunk = (16, 384)
-    new_weights, shown = pl.pallas_call(
-        kernel,
+    tail = tail.reshape(1, 1)
+    kept = pl.pallas_call(
+        functools.partial(kernel, ORDER),
         out_shape=[
-            jax.ShapeDtypeStruct((2048, 512), BF),
-            jax.ShapeDtypeStruct((2, 8, 512), F32),
+            pltpu.VMEM((2048, 768), BF),
+            pltpu.VMEM((2048, 512), F32),
+            pltpu.VMEM((2048, 256), BF),
+            pltpu.VMEM((256, 512), BF),
+            pltpu.VMEM((256, 512), BF),
+            pltpu.VMEM((2, 8, 512), F32),
         ],
         in_specs=[hbm] * 5 + [vmem] * 3,
-        out_specs=[hbm, hbm],
+        out_specs=[vmem] * 6,
         scratch_shapes=[
-            pltpu.VMEM((2, 512, 440), BF),
+            pltpu.VMEM((2, 440, 512), BF),
             pltpu.VMEM((440, 2048), BF),
-            pltpu.VMEM((2048, 768), BF),
             pltpu.VMEM((2, 512, 384), BF),
             pltpu.VMEM((2, 1, 384), F32),
             pltpu.VMEM((NP, 256, 2048), BF),
-            pltpu.VMEM((NP, 2048, 256), BF),
-            pltpu.VMEM((2048, 512), F32),
+            pltpu.VMEM((NP - 1, 2048, 256), BF),
             pltpu.VMEM((NP, 128, 768), F32),
             pltpu.VMEM((NP, 128, 768), BF),
             pltpu.VMEM((NP, 128, 768), BF),
@@ -351,9 +342,7 @@
             pltpu.VMEM((NP, 8) + chunk, BF),
             pltpu.VMEM((NP, 2, 16) + chunk, BF),
             pltpu.VMEM((NP, 256, 768), BF),
-            pltpu.VMEM((2048, 512), BF),
-            pltpu.VMEM((2, 8, 512), F32),
-            dma((6,)), dma((6,)),
+            dma((6,)),
             dma, dma,
             dma((NP,)), dma((NP,)),
             dma((NP, 3)), dma((NP, 3)),
@@ -364,15 +353,23 @@
             dma((NP,)), dma((NP,)),
         ],
         compiler_params=pltpu.CompilerParams(
-            collective_id=0, has_side_effects=True, vmem_limit_bytes=60 << 20
+            collective_id=0, has_side_effects=True, vmem_limit_bytes=48 << 20
         ),
         name="step",
     )(
-        inputs, targets, frequencies, weights, eigvecs,
-        phases.reshape(1, -1), eigvals.reshape(1, -1), tail.reshape(1, 1),
+        inputs.T, targets, frequencies, weights, eigvecs,
+        phases.reshape(1, -1), eigvals.reshape(1, -1), tail,
     )
-    residual = shown[:, 0:2, :].transpose(0, 2, 1).reshape(1024, 2)
-    return (new_weights, residual)
+    new_weights, residual = pl.pallas_call(
+        finish,
+        out_shape=[jax.ShapeDtypeStruct((2048, 512), BF), jax.ShapeDtypeStruct((2, 1024), F32)],
+        in_specs=[vmem] * 7,
+        out_specs=[hbm, vmem],
+        scratch_shapes=[pltpu.VMEM((2048, 512), BF), dma((4,))],
+        compiler_params=pltpu.CompilerParams(vmem_limit_bytes=16 << 20),
+        name="finish",
+    )(*kept, tail)
+    return (new_weights, residual.T)
 
 
 def solution(mesh):

time: 61.2 us -> 55.5 us (0.907)
  local copies, waits for them, and re-layouts: 6.42 us -> 0 us
  Pallas kernels: 53.3 us -> 54.1 us
    unnamed x2 -> x0, local copies, waits for them, and re-layouts: 5.06 us -> none
    slice x1 -> x0, local copies, waits for them, and re-layouts: 1.36 us -> none  [shards(): residual = shown[:, 0:2, :].transpose(0, 2, 1).reshape(1024, 2)]
    pallas_call x1 -> x2, Pallas kernels: 53.3 us -> 54.1 us  [the longest x1 50.8 us: shards(): pl.pallas_call(functools.partial(kernel, ORDER), out_shape=[pltpu.VMEM((2...]
where the time goes in v2:
time: 55.5 us; the launch traced here: 55.4 us
  Pallas kernels  54.1 us (97%)
  between operations  1.29 us (2%)
    pallas_call x1, Pallas kernels, shards(): pl.pallas_call(functools.partial(kernel, ORDER), out_shape=[pltpu.VMEM((2...  50.8 us
    pallas_call x1, Pallas kernels, shards(): pl.pallas_call(finish, out_shape=[jax.ShapeDtypeStruct((2048, 512), BF),...  3.29 us

profile of v2, /device:TPU:1, one launch (start us, length us, event | category | flops | bytes accessed | tf_op | source)
XLA Modules:
  0.0 55.4 jit_solution(5222032431056737803)
XLA Ops:
  1.3 50.8 %step.1 = (bf16[2048,768]{1,0:T(8,128)(2,1)S(1)}, f32[2048,512]{1,0:T(8,128)S(1)}, bf16[2048,256]{1,0:T(8,128)(2,1)S(1)}, bf16[256,512]{1,0:T(8,128)(2,1)S(1)}, ...) custom-call(bf16[440,512]{1,0:T(8,128)(2,1)} %bitcast.7, bf16[512,512]{1,0:T(8,128)(2,1)} %targ_hbm.1, ...), custom_call_target="tpu_custom_call" | custom-call | tf_op jit(solution)/shard_map/step/pallas_call | solution.py:315
  52.1 3.3 %finish.1 = (bf16[2048,512]{1,0:T(8,128)(2,1)}, f32[2,1024]{1,0:T(2,128)}) custom-call(bf16[2048,768]{1,0:T(8,128)(2,1)S(1)} %get-tuple-element.10.we_v, f32[2048,512]{1,0:T(8,128)S(1)} %get-tuple-element.11.g_v, bf16[2048,256]{1,0:T(8,128)(2,1)S(1)} %get-tuple-element.12.ft_last, bf16[256,512]{1,0:T(8,128)(2,1)S(1)} %get-tuple-element.13.resid_last, ...), custom_call_target="tpu_custom_call" | custom-call | tf_op jit(solution)/shard_map/finish/pallas_call | solution.py:363

commit v3 on v2

v3 whole, which is shorter than its diff:
```python
import functools
import math

import jax
import jax.numpy as jnp
from jax import lax
from jax.experimental import pallas as pl
from jax.experimental.pallas import tpu as pltpu
from jax.sharding import PartitionSpec as P

MESH = pl.DeviceIdType.MESH
BF, F32 = jnp.bfloat16, jnp.float32
FEATURES = 524288
SCALE = math.sqrt(2.0 / FEATURES)
INV_TURN = 1.0 / (2.0 * math.pi)
SIN = (6.283164044300404, -41.33714237083565, 81.34076887918835, -70.99343319450264)
NP = 4


def scaled_cos(theta, turns):
    t = theta * INV_TURN + turns
    s = 0.25 - jnp.abs(t - jnp.round(t))
    u = s * s
    p = SIN[3] * SCALE
    for q in SIN[2::-1]:
        p = p * u + q * SCALE
    return (s * p).astype(BF)


def kernel(
    order, in_hbm, targ_hbm, freq_hbm, w_hbm, e_hbm, phase_hbm, eig_hbm, tail_hbm,
    we_v, g_v, ft_last, resid_last, coeff_last, res_v, rate_v,
    x_v, freq_v, targ_v, scale_v, feat_v, ft_v, coeff_v, phase_v, eig_v, tail_v,
    xt_v, own_v, send_c, recv_c, buf_a, recv_a, recv_z, gath, rk_v,
    load_sem, sx, rx, sc, rc, sa, ra, sz, rz, sg, rg, sgc, rgc,
):
    f, c = lax.axis_index("feat"), lax.axis_index("rep")
    z, x, y = f // 16, (f // 4) % 4, f % 4

    def in_plane(d):
        i, j = (x + d // 4) % 4, (y + d % 4) % 4
        return 4 * i + j, (z * 16 + 4 * i + j, c)

    def at_z(d):
        return (((z + d) % 8) * 16 + x * 4 + y, c)

    mate = (f, 1 - c)
    barrier = pltpu.get_barrier_semaphore()
    everyone = [mate] + [in_plane(d)[1] for d in range(1, 16)] + [at_z(d) for d in range(1, 8)]
    loads = [
        (in_hbm, x_v.at[0]),
        (phase_hbm, phase_v),
        (freq_hbm, freq_v),
        (w_hbm, we_v.at[:, 0:512]),
        (e_hbm, we_v.at[:, 512:768]),
        (eig_hbm, eig_v),
        (tail_hbm, tail_v),
        (targ_hbm.at[:, 0:384], targ_v.at[0]),
        (targ_hbm.at[:, 384:512], targ_v.at[1, :, 0:128]),
    ]
    loads = [pltpu.make_async_copy(s, d, load_sem.at[i]) for i, (s, d) in enumerate(loads)]
    for load in loads:
        load.start()
    for peer in everyone:
        pl.semaphore_signal(barrier, inc=1, device_id=peer, device_id_type=MESH)

    def remote(src, dst, send, recv, peer):
        return pltpu.make_async_remote_copy(
            src_ref=src, dst_ref=dst, send_sem=send, recv_sem=recv,
            device_id=peer, device_id_type=MESH,
        )

    slot = 4 * x + y

    def core_copy(p):
        return remote(send_c.at[p], recv_c.at[p], sc.at[p], rc.at[p], mate)

    def a_copies(p):
        copies = []
        for d in range(1, 16):
            there, peer = in_plane(d)
            copies.append(remote(buf_a.at[p, there], recv_a.at[p, d - 1], sa.at[p, d - 1], ra.at[p, d - 1], peer))
        return copies

    def z_copies(p):
        here = recv_z.at[p, z]
        return [remote(here, here, sz.at[p, d - 1], rz.at[p, d - 1], at_z(d)) for d in range(1, 8)]

    def g_copies(p):
        here = gath.at[p, 0, slot]
        return [remote(here, here, sg.at[p, d - 1], rg.at[p, d - 1], in_plane(d)[1]) for d in range(1, 16)]

    def gc_copy(p):
        return remote(gath.at[p, 0], gath.at[p, 1], sgc.at[p], rgc.at[p], mate)

    def start(copies):
        for copy in copies:
            copy.start()

    def arrived(copies):
        for copy in copies:
            copy.wait_recv()

    def sent(copies):
        for copy in copies:
            copy.wait_send()

    def turn_inputs(half):
        for i in range(4):
            xt_v[half, i * 128:(i + 1) * 128, :] = x_v[half, :, i * 128:(i + 1) * 128].T

    def features(half, rows):
        for n in range(4):
            cols = slice(n * 512, (n + 1) * 512)
            theta = jnp.dot(xt_v[half, rows, :], freq_v[:, cols], preferred_element_type=F32)
            feat_v[half, rows, cols] = scaled_cos(theta, phase_v[:, cols] * INV_TURN)

    def own_features(n):
        turn_inputs(0)
        features(0, slice(0, 512))

    def mate_features(p):
        features(1, slice(p * 128, (p + 1) * 128))

    def own_project(n):
        rows = slice(n * 256, (n + 1) * 256)
        own_v[rows, :] = jnp.dot(feat_v[0, rows, :], we_v[...], preferred_element_type=F32)

    def mate_project(p):
        part = jnp.dot(feat_v[1, p * 128:(p + 1) * 128, :], we_v[...], preferred_element_type=F32)
        send_c[p] = part.astype(BF)
        core_copy(p).start()

    def stage_core(p):
        arrived([core_copy(p)])
        for i in range(8):
            rows = pl.ds(16 * i, 16)
            here = pl.ds(128 * p + 16 * i, 16)
            total = own_v[here, :] + recv_c[p, rows, :].astype(F32)
            own_v[here, :] = total
            for k in range(2):
                buf_a[p, 2 * i + k] = total[:, 384 * k:384 * (k + 1)].astype(BF)
        start(a_copies(p))
        sent([core_copy(p)])

    def chunk(ref, first_row):
        rows = pl.ds(pl.multiple_of(first_row + 16 * (slot // 2), 16), 16)
        cols = pl.ds(pl.multiple_of(384 * (slot % 2), 128), 384)
        return ref[rows, cols]

    def stage_plane(p):
        arrived(a_copies(p))
        total = chunk(own_v, 128 * p)
        for d in range(15):
            total = total + recv_a[p, d].astype(F32)
        recv_z[p, z] = total.astype(BF)
        start(z_copies(p))
        sent(a_copies(p))

    def stage_line(p):
        arrived(z_copies(p))
        total = recv_z[p, 0].astype(F32)
        for d in range(1, 8):
            total = total + recv_z[p, d].astype(F32)
        rows = pl.ds(pl.multiple_of(p * 128 + 16 * (slot // 2), 16), 16)
        total = total * scale_v[slot % 2] - targ_v[slot % 2, rows, :].astype(F32)
        gath[p, 0, slot] = total.astype(BF)
        start(g_copies(p))
        sent(z_copies(p))

    def stage_gather(p):
        arrived(g_copies(p))
        gc_copy(p).start()
        sent(g_copies(p))

    column = 4 * f + 2 * c

    def stage_last(p):
        arrived([gc_copy(p)])
        for half in range(2):
            for b in range(16):
                rows = 256 * p + 128 * half + 16 * (b // 2)
                rk_v[rows:rows + 16, 384 * (b % 2):384 * (b % 2 + 1)] = gath[p, half, b]
        sent([gc_copy(p)])
        resid = rk_v[256 * p:256 * (p + 1), 0:512]
        pick = lax.broadcasted_iota(jnp.int32, (8, 512), 1) == lax.broadcasted_iota(jnp.int32, (8, 512), 0) + column
        pick = jnp.where(pick, 1.0, 0.0).astype(BF)
        shown = lax.dot_general(pick, resid, (((1,), (1,)), ((), ())), preferred_element_type=F32)
        for half in range(2):
            res_v[half, :, p * 128:(p + 1) * 128] = shown[:, half * 128:(half + 1) * 128]
        coeff = lax.dot_general(
            rk_v[256 * p:256 * (p + 1), 512:768], resid, (((0,), (0,)), ((), ())), preferred_element_type=F32
        )
        if p > 0:
            coeff = coeff + coeff_v[...]
        if p < NP - 1:
            coeff_v[...] = coeff
        else:
            coeff_last[...] = (-coeff).astype(BF)
            resid_last[...] = resid

    def gradient(n):
        depth = pl.ds(0, 512) if n == 0 else pl.ds(512, 256)

        def tile(i, carry):
            rows = pl.ds(pl.multiple_of(i * 512, 512), 512)
            part = jnp.dot(ft_v[rows, depth], rk_v[depth, 0:512], preferred_element_type=F32)
            g_v[rows, :] = part if n == 0 else part + g_v[rows, :]
            return carry

        lax.fori_loop(0, 4, tile, 0)

    def flip(p):
        def tile(n, carry):
            cols = pl.ds(pl.multiple_of(n * 256, 256), 256)
            for half in range(2):
                turned = feat_v[half, p * 128:(p + 1) * 128, cols].T
                if p == NP - 1:
                    ft_last[cols, half * 128:(half + 1) * 128] = turned
                else:
                    ft_v[cols, p * 256 + half * 128:p * 256 + (half + 1) * 128] = turned
            return carry

        lax.fori_loop(0, 8, tile, 0)

    trade = remote(in_hbm, x_v.at[1], sx, rx, mate)

    def ready(n):
        if n == 0:
            for load in loads[0:3]:
                load.wait()
            targ_v[1, :, 128:384] = jnp.zeros((512, 256), BF)
        else:
            for load in loads[3:]:
                load.wait()
            scale_v[...] = jnp.ones_like(scale_v)
            scale_v[1, :, 128:384] = 1.0 - tail_v[...] / eig_v[...]
            rate_v[...] = jnp.broadcast_to(1.0 / tail_v[...], (1, 512))

    def greet(n):
        pl.semaphore_wait(barrier, len(everyone))
        trade.start()

    def meet(n):
        trade.wait()
        turn_inputs(1)

    steps = dict(
        L=ready, B=greet, T=meet, F=own_features, O=own_project, M=mate_features, P=mate_project,
        X=flip, a=stage_core, b=stage_plane, d=stage_line, f=stage_gather, g=stage_last, G=gradient,
    )
    for op in " ".join(order).split():
        steps[op[0]](int(op[1:]))


def finish(
    we_v, g_v, ft_last, resid_last, coeff_last, shown_v, rate_v,
    out_hbm, res_hbm, out_v, res_v, store_sem,
):
    c = lax.axis_index("rep")
    res_v[:, pl.ds(pl.multiple_of(c * 512, 512), 512)] = shown_v[0, 0:2, :]
    res_v[:, pl.ds(pl.multiple_of((1 - c) * 512, 512), 512)] = shown_v[1, 0:2, :]
    show = pltpu.make_async_copy(res_v, res_hbm, store_sem.at[4])
    show.start()

    def tile(n, carry):
        rows = pl.ds(pl.multiple_of(n * 512, 512), 512)
        part = jnp.dot(ft_last[rows, :], resid_last[...], preferred_element_type=F32)
        part = part + jnp.dot(we_v[rows, 512:768], coeff_last[...], preferred_element_type=F32)
        part = part + g_v[rows, :]
        out_v[rows, :] = (we_v[rows, 0:512].astype(F32) - part * rate_v[...]).astype(BF)
        pltpu.make_async_copy(out_v.at[rows], out_hbm.at[rows], store_sem.at[n]).start()
        return carry

    lax.fori_loop(0, 4, tile, 0)
    for n in range(4):
        rows = pl.ds(n * 512, 512)
        pltpu.make_async_copy(out_v.at[rows], out_hbm.at[rows], store_sem.at[n]).wait()
    show.wait()


ORDER = (
    "L0 F0 B0 L1", "O0 T0 M0 P0", "O1 a0 M1 P1", "M2 P2 a1", "M3 P3 a2", "X0 a3 X1", "b0 X2 b1 X3", "b2 b3 d0 d1",
    "d2 d3 f0 f1", "g0 f2 g1 f3", "G0 g2 G1 g3",
)


def shards(inputs, targets, frequencies, phases, weights, eigvecs, eigvals, tail):
    hbm = pl.BlockSpec(memory_space=pl.ANY)
    vmem = pl.BlockSpec(memory_space=pltpu.VMEM)
    dma = pltpu.SemaphoreType.DMA
    chunk = (16, 384)
    kept = pl.pallas_call(
        functools.partial(kernel, ORDER),
        out_shape=[
            pltpu.VMEM((2048, 768), BF),
            pltpu.VMEM((2048, 512), F32),
            pltpu.VMEM((2048, 256), BF),
            pltpu.VMEM((256, 512), BF),
            pltpu.VMEM((256, 512), BF),
            pltpu.VMEM((2, 8, 512), F32),
            pltpu.VMEM((1, 512), F32),
        ],
        in_specs=[hbm] * 8,
        out_specs=[vmem] * 7,
        scratch_shapes=[
            pltpu.VMEM((2, 440, 512), BF),
            pltpu.VMEM((440, 2048), BF),
            pltpu.VMEM((2, 512, 384), BF),
            pltpu.VMEM((2, 1, 384), F32),
            pltpu.VMEM((2, 512, 2048), BF),
            pltpu.VMEM((2048, 768), BF),
            pltpu.VMEM((256, 512), F32),
            pltpu.VMEM((1, 2048), F32),
            pltpu.VMEM((1, 256), F32),
            pltpu.VMEM((1, 1), F32),
            pltpu.VMEM((2, 512, 440), BF),
            pltpu.VMEM((512, 768), F32),
            pltpu.VMEM((NP, 128, 768), BF),
            pltpu.VMEM((NP, 128, 768), BF),
            pltpu.VMEM((NP, 16) + chunk, BF),
            pltpu.VMEM((NP, 15) + chunk, BF),
            pltpu.VMEM((NP, 8) + chunk, BF),
            pltpu.VMEM((NP, 2, 16) + chunk, BF),
            pltpu.VMEM((1024, 768), BF),
            dma((9,)),
            dma, dma,
            dma((NP,)), dma((NP,)),
            dma((NP, 15)), dma((NP, 15)),
            dma((NP, 7)), dma((NP, 7)),
            dma((NP, 15)), dma((NP, 15)),
            dma((NP,)), dma((NP,)),
        ],
        compiler_params=pltpu.CompilerParams(
            collective_id=0, has_side_effects=True, vmem_limit_bytes=48 << 20
        ),
        name="step",
    )(
        inputs.T, targets, frequencies, weights, eigvecs,
        phases.reshape(1, -1), eigvals.reshape(1, -1), tail.reshape(1, 1),
    )
    new_weights, residual = pl.pallas_call(
        finish,
        out_shape=[jax.ShapeDtypeStruct((2048, 512), BF), jax.ShapeDtypeStruct((2, 1024), F32)],
        in_specs=[vmem] * 7,
        out_specs=[hbm, hbm],
        scratch_shapes=[pltpu.VMEM((2048, 512), BF), pltpu.VMEM((2, 1024), F32), dma((5,))],
        compiler_params=pltpu.CompilerParams(vmem_limit_bytes=16 << 20),
        name="finish",
    )(*kept)
    return (new_weights, residual.T)


def solution(mesh):
    in_specs = (
        P("rep", None),
        P("rep", None),
        P(None, ("feat", "rep")),
        P(("feat", "rep")),
        P(("feat", "rep"), None),
        P(("feat", "rep"), None),
        P(),
        P(),
    )
    out_specs = (P(("feat", "rep"), None), P(None, ("feat", "rep")))
    return jax.shard_map(shards, mesh=mesh, in_specs=in_specs, out_specs=out_specs, check_vma=False)
```

time: 55.5 us -> 50.5 us (0.910)
  Pallas kernels: 54.1 us -> 49 us
    pallas_call x1, Pallas kernels: 50.8 us -> 46.3 us  [shards(): pl.pallas_call(functools.partial(kernel, ORDER), out_shape=[pltpu.VMEM((2...]
    pallas_call x1, Pallas kernels: 3.29 us -> 2.71 us  [shards(): pl.pallas_call(finish, out_shape=[jax.ShapeDtypeStruct((2048, 512), BF),...]
where the time goes in v3:
time: 50.5 us; the launch traced here: 50.4 us
  Pallas kernels  49 us (97%)
  between operations  1.45 us (3%)
    pallas_call x1, Pallas kernels, shards(): pl.pallas_call(functools.partial(kernel, ORDER), out_shape=[pltpu.VMEM((2...  46.3 us
    pallas_call x1, Pallas kernels, shards(): pl.pallas_call(finish, out_shape=[jax.ShapeDtypeStruct((2048, 512), BF),...  2.71 us

profile of v3, /device:TPU:1, one launch (start us, length us, event | category | flops | bytes accessed | tf_op | source)
XLA Modules:
  0.0 50.4 jit_solution(6518282900638935709)
XLA Ops:
  1.3 46.3 %step.1 = (bf16[2048,768]{1,0:T(8,128)(2,1)S(1)}, f32[2048,512]{1,0:T(8,128)S(1)}, bf16[2048,256]{1,0:T(8,128)(2,1)S(1)}, bf16[256,512]{1,0:T(8,128)(2,1)S(1)}, ...) custom-call(bf16[440,512]{1,0:T(8,128)(2,1)} %bitcast.6, bf16[512,512]{1,0:T(8,128)(2,1)} %targ_hbm.1, ...), custom_call_target="tpu_custom_call" | custom-call | tf_op jit(solution)/shard_map/step/pallas_call | solution.py:293
  47.6 2.7 %finish.1 = (bf16[2048,512]{1,0:T(8,128)(2,1)}, f32[2,1024]{1,0:T(2,128)}) custom-call(bf16[2048,768]{1,0:T(8,128)(2,1)S(1)} %get-tuple-element.11.we_v, f32[2048,512]{1,0:T(8,128)S(1)} %get-tuple-element.12.g_v, bf16[2048,256]{1,0:T(8,128)(2,1)S(1)} %get-tuple-element.13.ft_last, bf16[256,512]{1,0:T(8,128)(2,1)S(1)} %get-tuple-element.14.resid_last, ...), custom_call_target="tpu_custom_call" | custom-call | tf_op jit(solution)/shard_map/finish/pallas_call | solution.py:342

commit v4 on v3

--- a/solution.py
+++ b/solution.py
@@ -79,16 +79,27 @@
         copies = []
         for d in range(1, 16):
             there, peer = in_plane(d)
-            copies.append(remote(buf_a.at[p, there], recv_a.at[p, d - 1], sa.at[p, d - 1], ra.at[p, d - 1], peer))
+            copies.append(remote(buf_a.at[p, there], recv_a.at[p, d - 1], sa.at[p], ra.at[p], peer))
         return copies
 
     def z_copies(p):
         here = recv_z.at[p, z]
-        return [remote(here, here, sz.at[p, d - 1], rz.at[p, d - 1], at_z(d)) for d in range(1, 8)]
+        return [remote(here, here, sz.at[p], rz.at[p], at_z(d)) for d in range(1, 8)]
 
     def g_copies(p):
         here = gath.at[p, 0, slot]
-        return [remote(here, here, sg.at[p, d - 1], rg.at[p, d - 1], in_plane(d)[1]) for d in range(1, 16)]
+        return [remote(here, here, sg.at[p], rg.at[p], in_plane(d)[1]) for d in range(1, 16)]
+
+    def a_all(p):
+        return remote(recv_a.at[p], recv_a.at[p], sa.at[p], ra.at[p], mate)
+
+    def z_all(p):
+        here = recv_z.at[p, 0:7]
+        return remote(here, here, sz.at[p], rz.at[p], mate)
+
+    def g_all(p):
+        here = gath.at[p, 0, 0:15]
+        return remote(here, here, sg.at[p], rg.at[p], mate)
 
     def gc_copy(p):
         return remote(gath.at[p, 0], gath.at[p, 1], sgc.at[p], rgc.at[p], mate)
@@ -96,14 +107,6 @@
     def start(copies):
         for copy in copies:
             copy.start()
-
-    def arrived(copies):
-        for copy in copies:
-            copy.wait_recv()
-
-    def sent(copies):
-        for copy in copies:
-            copy.wait_send()
 
     def turn_inputs(half):
         for i in range(4):
@@ -132,7 +135,7 @@
         core_copy(p).start()
 
     def stage_core(p):
-        arrived([core_copy(p)])
+        core_copy(p).wait_recv()
         for i in range(8):
             rows = pl.ds(16 * i, 16)
             here = pl.ds(128 * p + 16 * i, 16)
@@ -141,7 +144,7 @@
             for k in range(2):
                 buf_a[p, 2 * i + k] = total[:, 384 * k:384 * (k + 1)].astype(BF)
         start(a_copies(p))
-        sent([core_copy(p)])
+        core_copy(p).wait_send()
 
     def chunk(ref, first_row):
         rows = pl.ds(pl.multiple_of(first_row + 16 * (slot // 2), 16), 16)
@@ -149,16 +152,16 @@
         return ref[rows, cols]
 
     def stage_plane(p):
-        arrived(a_copies(p))
+        a_all(p).wait_recv()
         total = chunk(own_v, 128 * p)
         for d in range(15):
             total = total + recv_a[p, d].astype(F32)
         recv_z[p, z] = total.astype(BF)
         start(z_copies(p))
-        sent(a_copies(p))
+        a_all(p).wait_send()
 
     def stage_line(p):
-        arrived(z_copies(p))
+        z_all(p).wait_recv()
         total = recv_z[p, 0].astype(F32)
         for d in range(1, 8):
             total = total + recv_z[p, d].astype(F32)
@@ -166,22 +169,22 @@
         total = total * scale_v[slot % 2] - targ_v[slot % 2, rows, :].astype(F32)
         gath[p, 0, slot] = total.astype(BF)
         start(g_copies(p))
-        sent(z_copies(p))
+        z_all(p).wait_send()
 
     def stage_gather(p):
-        arrived(g_copies(p))
+        g_all(p).wait_recv()
         gc_copy(p).start()
-        sent(g_copies(p))
+        g_all(p).wait_send()
 
     column = 4 * f + 2 * c
 
     def stage_last(p):
-        arrived([gc_copy(p)])
+        gc_copy(p).wait_recv()
         for half in range(2):
             for b in range(16):
                 rows = 256 * p + 128 * half + 16 * (b // 2)
                 rk_v[rows:rows + 16, 384 * (b % 2):384 * (b % 2 + 1)] = gath[p, half, b]
-        sent([gc_copy(p)])
+        gc_copy(p).wait_send()
         resid = rk_v[256 * p:256 * (p + 1), 0:512]
         pick = lax.broadcasted_iota(jnp.int32, (8, 512), 1) == lax.broadcasted_iota(jnp.int32, (8, 512), 0) + column
         pick = jnp.where(pick, 1.0, 0.0).astype(BF)
@@ -234,8 +237,8 @@
             for load in loads[3:]:
                 load.wait()
             scale_v[...] = jnp.ones_like(scale_v)
-            scale_v[1, :, 128:384] = 1.0 - tail_v[...] / eig_v[...]
-            rate_v[...] = jnp.broadcast_to(1.0 / tail_v[...], (1, 512))
+            scale_v[1, :, 128:384] = 1.0 - tail_v[0] / eig_v[...]
+            rate_v[...] = 1.0 / jnp.full((1, 512), tail_v[0], F32)
 
     def greet(n):
         pl.semaphore_wait(barrier, len(everyone))
@@ -313,7 +316,7 @@
             pltpu.VMEM((256, 512), F32),
             pltpu.VMEM((1, 2048), F32),
             pltpu.VMEM((1, 256), F32),
-            pltpu.VMEM((1, 1), F32),
+            pltpu.SMEM((1,), F32),
             pltpu.VMEM((2, 512, 440), BF),
             pltpu.VMEM((512, 768), F32),
             pltpu.VMEM((NP, 128, 768), BF),
@@ -326,9 +329,9 @@
             dma((9,)),
             dma, dma,
             dma((NP,)), dma((NP,)),
-            dma((NP, 15)), dma((NP, 15)),
-            dma((NP, 7)), dma((NP, 7)),
-            dma((NP, 15)), dma((NP, 15)),
+            dma((NP,)), dma((NP,)),
+            dma((NP,)), dma((NP,)),
+            dma((NP,)), dma((NP,)),
             dma((NP,)), dma((NP,)),
         ],
         compiler_params=pltpu.CompilerParams(
@@ -337,7 +340,7 @@
         name="step",
     )(
         inputs.T, targets, frequencies, weights, eigvecs,
-        phases.reshape(1, -1), eigvals.reshape(1, -1), tail.reshape(1, 1),
+        phases.reshape(1, -1), eigvals.reshape(1, -1), tail,
     )
     new_weights, residual = pl.pallas_call(
         finish,

time: 50.5 us -> 47.8 us (0.947)
  Pallas kernels: 49 us -> 46.2 us
    pallas_call x1, Pallas kernels: 46.3 us -> 43.5 us  [shards(): pl.pallas_call(functools.partial(kernel, ORDER), out_shape=[pltpu.VMEM((2...]
where the time goes in v4:
time: 47.8 us; the launch traced here: 47.7 us
  Pallas kernels  46.2 us (97%)
  between operations  1.45 us (3%)
    pallas_call x1, Pallas kernels, shards(): pl.pallas_call(functools.partial(kernel, ORDER), out_shape=[pltpu.VMEM((2...  43.5 us
    pallas_call x1, Pallas kernels, shards(): pl.pallas_call(finish, out_shape=[jax.ShapeDtypeStruct((2048, 512), BF),...  2.71 us

profile of v4, /device:TPU:1, one launch (start us, length us, event | category | flops | bytes accessed | tf_op | source)
XLA Modules:
  0.0 47.7 jit_solution(9788229474074429500)
XLA Ops:
  1.3 43.5 %step.1 = (bf16[2048,768]{1,0:T(8,128)(2,1)S(1)}, f32[2048,512]{1,0:T(8,128)S(1)}, bf16[2048,256]{1,0:T(8,128)(2,1)S(1)}, bf16[256,512]{1,0:T(8,128)(2,1)S(1)}, ...) custom-call(bf16[440,512]{1,0:T(8,128)(2,1)} %bitcast.4, bf16[512,512]{1,0:T(8,128)(2,1)} %targ_hbm.1, ...), custom_call_target="tpu_custom_call" | custom-call | tf_op jit(solution)/shard_map/step/pallas_call | solution.py:296
  44.8 2.7 %finish.1 = (bf16[2048,512]{1,0:T(8,128)(2,1)}, f32[2,1024]{1,0:T(2,128)}) custom-call(bf16[2048,768]{1,0:T(8,128)(2,1)S(1)} %get-tuple-element.11.we_v, f32[2048,512]{1,0:T(8,128)S(1)} %get-tuple-element.12.g_v, bf16[2048,256]{1,0:T(8,128)(2,1)S(1)} %get-tuple-element.13.ft_last, bf16[256,512]{1,0:T(8,128)(2,1)S(1)} %get-tuple-element.14.resid_last, ...), custom_call_target="tpu_custom_call" | custom-call | tf_op jit(solution)/shard_map/finish/pallas_call | solution.py:345

commit v5 on v4

--- a/solution.py
+++ b/solution.py
@@ -29,7 +29,7 @@
 
 def kernel(
     order, in_hbm, targ_hbm, freq_hbm, w_hbm, e_hbm, phase_hbm, eig_hbm, tail_hbm,
-    we_v, g_v, ft_last, resid_last, coeff_last, res_v, rate_v,
+    w_v, ef_v, g_v, rc_last, res_v, rate_v,
     x_v, freq_v, targ_v, scale_v, feat_v, ft_v, coeff_v, phase_v, eig_v, tail_v,
     xt_v, own_v, send_c, recv_c, buf_a, recv_a, recv_z, gath, rk_v,
     load_sem, sx, rx, sc, rc, sa, ra, sz, rz, sg, rg, sgc, rgc,
@@ -51,8 +51,8 @@
         (in_hbm, x_v.at[0]),
         (phase_hbm, phase_v),
         (freq_hbm, freq_v),
-        (w_hbm, we_v.at[:, 0:512]),
-        (e_hbm, we_v.at[:, 512:768]),
+        (w_hbm, w_v),
+        (e_hbm, ef_v.at[:, 0:256]),
         (eig_hbm, eig_v),
         (tail_hbm, tail_v),
         (targ_hbm.at[:, 0:384], targ_v.at[0]),
@@ -118,20 +118,25 @@
             theta = jnp.dot(xt_v[half, rows, :], freq_v[:, cols], preferred_element_type=F32)
             feat_v[half, rows, cols] = scaled_cos(theta, phase_v[:, cols] * INV_TURN)
 
+    def project(half, rows):
+        feats = feat_v[half, rows, :]
+        on_w = jnp.dot(feats, w_v[...], preferred_element_type=F32)
+        return on_w, jnp.dot(feats, ef_v[:, 0:256], preferred_element_type=F32)
+
     def own_features(n):
-        turn_inputs(0)
         features(0, slice(0, 512))
+
+    def own_project(n):
+        rows = slice(n * 256, (n + 1) * 256)
+        own_v[rows, 0:512], own_v[rows, 512:768] = project(0, rows)
 
     def mate_features(p):
         features(1, slice(p * 128, (p + 1) * 128))
 
-    def own_project(n):
-        rows = slice(n * 256, (n + 1) * 256)
-        own_v[rows, :] = jnp.dot(feat_v[0, rows, :], we_v[...], preferred_element_type=F32)
-
     def mate_project(p):
-        part = jnp.dot(feat_v[1, p * 128:(p + 1) * 128, :], we_v[...], preferred_element_type=F32)
-        send_c[p] = part.astype(BF)
+        on_w, on_e = project(1, slice(p * 128, (p + 1) * 128))
+        send_c[p, :, 0:512] = on_w.astype(BF)
+        send_c[p, :, 512:768] = on_e.astype(BF)
         core_copy(p).start()
 
     def stage_core(p):
@@ -199,11 +204,11 @@
         if p < NP - 1:
             coeff_v[...] = coeff
         else:
-            coeff_last[...] = (-coeff).astype(BF)
-            resid_last[...] = resid
+            rc_last[0:256, :] = (-coeff).astype(BF)
+            rc_last[256:512, :] = resid
 
     def gradient(n):
-        depth = pl.ds(0, 512) if n == 0 else pl.ds(512, 256)
+        depth = pl.ds(0, 256) if n == 0 else pl.ds(256, 512)
 
         def tile(i, carry):
             rows = pl.ds(pl.multiple_of(i * 512, 512), 512)
@@ -219,7 +224,7 @@
             for half in range(2):
                 turned = feat_v[half, p * 128:(p + 1) * 128, cols].T
                 if p == NP - 1:
-                    ft_last[cols, half * 128:(half + 1) * 128] = turned
+                    ef_v[cols, 256 + half * 128:256 + (half + 1) * 128] = turned
                 else:
                     ft_v[cols, p * 256 + half * 128:p * 256 + (half + 1) * 128] = turned
             return carry
@@ -232,6 +237,7 @@
         if n == 0:
             for load in loads[0:3]:
                 load.wait()
+            turn_inputs(0)
             targ_v[1, :, 128:384] = jnp.zeros((512, 256), BF)
         else:
             for load in loads[3:]:
@@ -257,7 +263,7 @@
 
 
 def finish(
-    we_v, g_v, ft_last, resid_last, coeff_last, shown_v, rate_v,
+    w_v, ef_v, g_v, rc_last, shown_v, rate_v,
     out_hbm, res_hbm, out_v, res_v, store_sem,
 ):
     c = lax.axis_index("rep")
@@ -268,10 +274,8 @@
 
     def tile(n, carry):
         rows = pl.ds(pl.multiple_of(n * 512, 512), 512)
-        part = jnp.dot(ft_last[rows, :], resid_last[...], preferred_element_type=F32)
-        part = part + jnp.dot(we_v[rows, 512:768], coeff_last[...], preferred_element_type=F32)
-        part = part + g_v[rows, :]
-        out_v[rows, :] = (we_v[rows, 0:512].astype(F32) - part * rate_v[...]).astype(BF)
+        part = jnp.dot(ef_v[rows, :], rc_last[...], preferred_element_type=F32) + g_v[rows, :]
+        out_v[rows, :] = (w_v[rows, :].astype(F32) - part * rate_v[...]).astype(BF)
         pltpu.make_async_copy(out_v.at[rows], out_hbm.at[rows], store_sem.at[n]).start()
         return carry
 
@@ -283,8 +287,8 @@
 
 
 ORDER = (
-    "L0 F0 B0 L1", "O0 T0 M0 P0", "O1 a0 M1 P1", "M2 P2 a1", "M3 P3 a2", "X0 a3 X1", "b0 X2 b1 X3", "b2 b3 d0 d1",
-    "d2 d3 f0 f1", "g0 f2 g1 f3", "G0 g2 G1 g3",
+    "L0 L1 B0", "F0 O0 T0", "M0 P0 O1", "M1 P1 a0", "M2 P2 a1", "M3 P3 a2", "a3 X0 X1", "b0 X2 b1 X3", "b2 b3",
+    "d0 d1 d2 d3", "f0 f1 g0 G0", "f2 g1 f3 g2", "G1 g3",
 )
 
 
@@ -296,16 +300,15 @@
     kept = pl.pallas_call(
         functools.partial(kernel, ORDER),
         out_shape=[
-            pltpu.VMEM((2048, 768), BF),
+            pltpu.VMEM((2048, 512), BF),
+            pltpu.VMEM((2048, 512), BF),
             pltpu.VMEM((2048, 512), F32),
-            pltpu.VMEM((2048, 256), BF),
-            pltpu.VMEM((256, 512), BF),
-            pltpu.VMEM((256, 512), BF),
+            pltpu.VMEM((512, 512), BF),
             pltpu.VMEM((2, 8, 512), F32),
             pltpu.VMEM((1, 512), F32),
         ],
         in_specs=[hbm] * 8,
-        out_specs=[vmem] * 7,
+        out_specs=[vmem] * 6,
         scratch_shapes=[
             pltpu.VMEM((2, 440, 512), BF),
             pltpu.VMEM((440, 2048), BF),
@@ -345,7 +348,7 @@
     new_weights, residual = pl.pallas_call(
         finish,
         out_shape=[jax.ShapeDtypeStruct((2048, 512), BF), jax.ShapeDtypeStruct((2, 1024), F32)],
-        in_specs=[vmem] * 7,
+        in_specs=[vmem] * 6,
         out_specs=[hbm, hbm],
         scratch_shapes=[pltpu.VMEM((2048, 512), BF), pltpu.VMEM((2, 1024), F32), dma((5,))],
         compiler_params=pltpu.CompilerParams(vmem_limit_bytes=16 << 20),

time: 47.8 us -> 49.3 us (1.031)
  Pallas kernels: 46.2 us -> 47.9 us
    pallas_call x1, Pallas kernels: 43.5 us -> 45.2 us  [shards(): pl.pallas_call(functools.partial(kernel, ORDER), out_shape=[pltpu.VMEM((2...]
where the time goes in v5:
time: 49.3 us; the launch traced here: 49.2 us
  Pallas kernels  47.9 us (97%)
  between operations  1.29 us (3%)
    pallas_call x1, Pallas kernels, shards(): pl.pallas_call(functools.partial(kernel, ORDER), out_shape=[pltpu.VMEM((2...  45.2 us
    pallas_call x1, Pallas kernels, shards(): pl.pallas_call(finish, out_shape=[jax.ShapeDtypeStruct((2048, 512), BF),...  2.71 us

profile of v5, /device:TPU:1, one launch (start us, length us, event | category | flops | bytes accessed | tf_op | source)
XLA Modules:
  0.0 49.2 jit_solution(15612302231790644876)
XLA Ops:
  1.3 45.2 %step.1 = (bf16[2048,512]{1,0:T(8,128)(2,1)S(1)}, bf16[2048,512]{1,0:T(8,128)(2,1)S(1)}, f32[2048,512]{1,0:T(8,128)S(1)}, bf16[512,512]{1,0:T(8,128)(2,1)S(1)}, ...) custom-call(bf16[440,512]{1,0:T(8,128)(2,1)} %bitcast.4, bf16[512,512]{1,0:T(8,128)(2,1)} %targ_hbm.1, ...), custom_call_target="tpu_custom_call" | custom-call | tf_op jit(solution)/shard_map/step/pallas_call | solution.py:300
  46.5 2.7 %finish.1 = (bf16[2048,512]{1,0:T(8,128)(2,1)}, f32[2,1024]{1,0:T(2,128)}) custom-call(bf16[2048,512]{1,0:T(8,128)(2,1)S(1)} %get-tuple-element.10.w_v, bf16[2048,512]{1,0:T(8,128)(2,1)S(1)} %get-tuple-element.11.ef_v, f32[2048,512]{1,0:T(8,128)S(1)} %get-tuple-element.12.g_v, bf16[512,512]{1,0:T(8,128)(2,1)S(1)} %get-tuple-element.13.rc_last, ...), custom_call_target="tpu_custom_call" | custom-call | tf_op jit(solution)/shard_map/finish/pallas_call | solution.py:348

commit v6 on v5

--- a/solution.py
+++ b/solution.py
@@ -205,15 +205,12 @@
             coeff_v[...] = coeff
         else:
             rc_last[0:256, :] = (-coeff).astype(BF)
-            rc_last[256:512, :] = resid
+            rc_last[256:768, :] = rk_v[512:1024, 0:512]
 
     def gradient(n):
-        depth = pl.ds(0, 256) if n == 0 else pl.ds(256, 512)
-
         def tile(i, carry):
             rows = pl.ds(pl.multiple_of(i * 512, 512), 512)
-            part = jnp.dot(ft_v[rows, depth], rk_v[depth, 0:512], preferred_element_type=F32)
-            g_v[rows, :] = part if n == 0 else part + g_v[rows, :]
+            g_v[rows, :] = jnp.dot(ft_v[rows, :], rk_v[0:512, 0:512], preferred_element_type=F32)
             return carry
 
         lax.fori_loop(0, 4, tile, 0)
@@ -223,10 +220,10 @@
             cols = pl.ds(pl.multiple_of(n * 256, 256), 256)
             for half in range(2):
                 turned = feat_v[half, p * 128:(p + 1) * 128, cols].T
-                if p == NP - 1:
-                    ef_v[cols, 256 + half * 128:256 + (half + 1) * 128] = turned
+                if p < 2:
+                    ft_v[cols, p * 256 + half * 128:p * 256 + (half + 1) * 128] = turned
                 else:
-                    ft_v[cols, p * 256 + half * 128:p * 256 + (half + 1) * 128] = turned
+                    ef_v[cols, (p - 1) * 256 + half * 128:(p - 1) * 256 + (half + 1) * 128] = turned
             return carry
 
         lax.fori_loop(0, 8, tile, 0)
@@ -287,8 +284,8 @@
 
 
 ORDER = (
-    "L0 L1 B0", "F0 O0 T0", "M0 P0 O1", "M1 P1 a0", "M2 P2 a1", "M3 P3 a2", "a3 X0 X1", "b0 X2 b1 X3", "b2 b3",
-    "d0 d1 d2 d3", "f0 f1 g0 G0", "f2 g1 f3 g2", "G1 g3",
+    "L0 F0 B0 L1", "O0 T0 M0 P0", "O1 a0 M1 P1", "M2 P2 a1", "M3 P3 a2", "X0 a3 X1", "b0 X2 b1 X3", "b2 b3",
+    "d0 d1 d2 d3", "f0 f1 g0", "f2 g1 G0", "f3 g2 g3",
 )
 
 
@@ -301,9 +298,9 @@
         functools.partial(kernel, ORDER),
         out_shape=[
             pltpu.VMEM((2048, 512), BF),
-            pltpu.VMEM((2048, 512), BF),
+            pltpu.VMEM((2048, 768), BF),
             pltpu.VMEM((2048, 512), F32),
-            pltpu.VMEM((512, 512), BF),
+            pltpu.VMEM((768, 512), BF),
             pltpu.VMEM((2, 8, 512), F32),
             pltpu.VMEM((1, 512), F32),
         ],
@@ -315,7 +312,7 @@
             pltpu.VMEM((2, 512, 384), BF),
             pltpu.VMEM((2, 1, 384), F32),
             pltpu.VMEM((2, 512, 2048), BF),
-            pltpu.VMEM((2048, 768), BF),
+            pltpu.VMEM((2048, 512), BF),
             pltpu.VMEM((256, 512), F32),
             pltpu.VMEM((1, 2048), F32),
             pltpu.VMEM((1, 256), F32),

time: 49.3 us -> 48.4 us (0.982)
  Pallas kernels: 47.9 us -> 47 us
    pallas_call x1, Pallas kernels: 45.2 us -> 43.7 us  [shards(): pl.pallas_call(functools.partial(kernel, ORDER), out_shape=[pltpu.VMEM((2...]
    pallas_call x1, Pallas kernels: 2.71 us -> 3.25 us  [shards(): pl.pallas_call(finish, out_shape=[jax.ShapeDtypeStruct((2048, 512), BF),...]
where the time goes in v6:
time: 48.4 us; the launch traced here: 48.3 us
  Pallas kernels  47 us (97%)
  between operations  1.29 us (3%)
    pallas_call x1, Pallas kernels, shards(): pl.pallas_call(functools.partial(kernel, ORDER), out_shape=[pltpu.VMEM((2...  43.7 us
    pallas_call x1, Pallas kernels, shards(): pl.pallas_call(finish, out_shape=[jax.ShapeDtypeStruct((2048, 512), BF),...  3.25 us

profile of v6, /device:TPU:1, one launch (start us, length us, event | category | flops | bytes accessed | tf_op | source)
XLA Modules:
  0.0 48.3 jit_solution(1967352148101727012)
XLA Ops:
  1.3 43.7 %step.1 = (bf16[2048,512]{1,0:T(8,128)(2,1)S(1)}, bf16[2048,768]{1,0:T(8,128)(2,1)S(1)}, f32[2048,512]{1,0:T(8,128)S(1)}, bf16[768,512]{1,0:T(8,128)(2,1)S(1)}, ...) custom-call(bf16[440,512]{1,0:T(8,128)(2,1)} %bitcast.4, bf16[512,512]{1,0:T(8,128)(2,1)} %targ_hbm.1, ...), custom_call_target="tpu_custom_call" | custom-call | tf_op jit(solution)/shard_map/step/pallas_call | solution.py:297
  45.0 3.2 %finish.1 = (bf16[2048,512]{1,0:T(8,128)(2,1)}, f32[2,1024]{1,0:T(2,128)}) custom-call(bf16[2048,512]{1,0:T(8,128)(2,1)S(1)} %get-tuple-element.10.w_v, bf16[2048,768]{1,0:T(8,128)(2,1)S(1)} %get-tuple-element.11.ef_v, f32[2048,512]{1,0:T(8,128)S(1)} %get-tuple-element.12.g_v, bf16[768,512]{1,0:T(8,128)(2,1)S(1)} %get-tuple-element.13.rc_last, ...), custom_call_target="tpu_custom_call" | custom-call | tf_op jit(solution)/shard_map/finish/pallas_call | solution.py:345

commit v7 on v5

--- a/solution.py
+++ b/solution.py
@@ -208,15 +208,11 @@
             rc_last[256:512, :] = resid
 
     def gradient(n):
-        depth = pl.ds(0, 256) if n == 0 else pl.ds(256, 512)
-
-        def tile(i, carry):
-            rows = pl.ds(pl.multiple_of(i * 512, 512), 512)
+        depth = slice(0, 512) if n == 0 else slice(512, 768)
+        for i in range(8):
+            rows = slice(i * 256, (i + 1) * 256)
             part = jnp.dot(ft_v[rows, depth], rk_v[depth, 0:512], preferred_element_type=F32)
             g_v[rows, :] = part if n == 0 else part + g_v[rows, :]
-            return carry
-
-        lax.fori_loop(0, 4, tile, 0)
 
     def flip(p):
         def tile(n, carry):
@@ -269,26 +265,23 @@
     c = lax.axis_index("rep")
     res_v[:, pl.ds(pl.multiple_of(c * 512, 512), 512)] = shown_v[0, 0:2, :]
     res_v[:, pl.ds(pl.multiple_of((1 - c) * 512, 512), 512)] = shown_v[1, 0:2, :]
-    show = pltpu.make_async_copy(res_v, res_hbm, store_sem.at[4])
+    show = pltpu.make_async_copy(res_v, res_hbm, store_sem.at[8])
     show.start()
 
-    def tile(n, carry):
-        rows = pl.ds(pl.multiple_of(n * 512, 512), 512)
+    copies = [show]
+    for n in range(8):
+        rows = slice(n * 256, (n + 1) * 256)
         part = jnp.dot(ef_v[rows, :], rc_last[...], preferred_element_type=F32) + g_v[rows, :]
         out_v[rows, :] = (w_v[rows, :].astype(F32) - part * rate_v[...]).astype(BF)
-        pltpu.make_async_copy(out_v.at[rows], out_hbm.at[rows], store_sem.at[n]).start()
-        return carry
-
-    lax.fori_loop(0, 4, tile, 0)
-    for n in range(4):
-        rows = pl.ds(n * 512, 512)
-        pltpu.make_async_copy(out_v.at[rows], out_hbm.at[rows], store_sem.at[n]).wait()
-    show.wait()
+        copies.append(pltpu.make_async_copy(out_v.at[rows], out_hbm.at[rows], store_sem.at[n]))
+        copies[-1].start()
+    for copy in copies:
+        copy.wait()
 
 
 ORDER = (
-    "L0 L1 B0", "F0 O0 T0", "M0 P0 O1", "M1 P1 a0", "M2 P2 a1", "M3 P3 a2", "a3 X0 X1", "b0 X2 b1 X3", "b2 b3",
-    "d0 d1 d2 d3", "f0 f1 g0 G0", "f2 g1 f3 g2", "G1 g3",
+    "L0 F0 B0 L1", "O0 T0 M0 P0", "O1 a0 M1 P1", "M2 P2 a1", "M3 P3 a2", "X0 a3 X1", "b0 X2 b1 X3", "b2 b3",
+    "d0 d1 d2 d3", "f0 f1 g0", "f2 g1 G0", "f3 g2 G1 g3",
 )
 
 
@@ -350,7 +343,7 @@
         out_shape=[jax.ShapeDtypeStruct((2048, 512), BF), jax.ShapeDtypeStruct((2, 1024), F32)],
         in_specs=[vmem] * 6,
         out_specs=[hbm, hbm],
-        scratch_shapes=[pltpu.VMEM((2048, 512), BF), pltpu.VMEM((2, 1024), F32), dma((5,))],
+        scratch_shapes=[pltpu.VMEM((2048, 512), BF), pltpu.VMEM((2, 1024), F32), dma((9,))],
         compiler_params=pltpu.CompilerParams(vmem_limit_bytes=16 << 20),
         name="finish",
     )(*kept)

time: 49.3 us -> 47.5 us (0.963)
  Pallas kernels: 47.9 us -> 45.9 us
    pallas_call x1, Pallas kernels: 45.2 us -> 43.8 us  [shards(): pl.pallas_call(functools.partial(kernel, ORDER), out_shape=[pltpu.VMEM((2...]
    pallas_call x1, Pallas kernels: 2.71 us -> 2.11 us  [shards(): pl.pallas_call(finish, out_shape=[jax.ShapeDtypeStruct((2048, 512), BF),...]
where the time goes in v7:
time: 47.5 us; the launch traced here: 47.4 us
  Pallas kernels  45.9 us (97%)
  between operations  1.45 us (3%)
    pallas_call x1, Pallas kernels, shards(): pl.pallas_call(functools.partial(kernel, ORDER), out_shape=[pltpu.VMEM((2...  43.8 us
    pallas_call x1, Pallas kernels, shards(): pl.pallas_call(finish, out_shape=[jax.ShapeDtypeStruct((2048, 512), BF),...  2.11 us

profile of v7, /device:TPU:1, one launch (start us, length us, event | category | flops | bytes accessed | tf_op | source)
XLA Modules:
  0.0 47.4 jit_solution(10419539911325413527)
XLA Ops:
  1.3 43.8 %step.1 = (bf16[2048,512]{1,0:T(8,128)(2,1)S(1)}, bf16[2048,512]{1,0:T(8,128)(2,1)S(1)}, f32[2048,512]{1,0:T(8,128)S(1)}, bf16[512,512]{1,0:T(8,128)(2,1)S(1)}, ...) custom-call(bf16[440,512]{1,0:T(8,128)(2,1)} %bitcast.4, bf16[512,512]{1,0:T(8,128)(2,1)} %targ_hbm.1, ...), custom_call_target="tpu_custom_call" | custom-call | tf_op jit(solution)/shard_map/step/pallas_call | solution.py:293
  45.1 2.1 %finish.1 = (bf16[2048,512]{1,0:T(8,128)(2,1)}, f32[2,1024]{1,0:T(2,128)}) custom-call(bf16[2048,512]{1,0:T(8,128)(2,1)S(1)} %get-tuple-element.10.w_v, bf16[2048,512]{1,0:T(8,128)(2,1)S(1)} %get-tuple-element.11.ef_v, f32[2048,512]{1,0:T(8,128)S(1)} %get-tuple-element.12.g_v, bf16[512,512]{1,0:T(8,128)(2,1)S(1)} %get-tuple-element.13.rc_last, ...), custom_call_target="tpu_custom_call" | custom-call | tf_op jit(solution)/shard_map/finish/pallas_call | solution.py:341

commit v8 on v7

--- a/solution.py
+++ b/solution.py
@@ -127,7 +127,7 @@
         features(0, slice(0, 512))
 
     def own_project(n):
-        rows = slice(n * 256, (n + 1) * 256)
+        rows = slice(n * 128, (n + 1) * 128)
         own_v[rows, 0:512], own_v[rows, 512:768] = project(0, rows)
 
     def mate_features(p):
@@ -280,7 +280,7 @@
 
 
 ORDER = (
-    "L0 F0 B0 L1", "O0 T0 M0 P0", "O1 a0 M1 P1", "M2 P2 a1", "M3 P3 a2", "X0 a3 X1", "b0 X2 b1 X3", "b2 b3",
+    "L0 F0 B0 L1", "O0 O1 T0 M0", "P0 M1 P1 a0", "M2 P2 a1 O2", "M3 P3 a2 O3", "a3 X0 X1 b0", "X2 b1 X3 b2", "b3",
     "d0 d1 d2 d3", "f0 f1 g0", "f2 g1 G0", "f3 g2 G1 g3",
 )
 

time: 47.5 us -> 46.9 us (0.987)
  Pallas kernels: 45.9 us -> 45.3 us
    pallas_call x1, Pallas kernels: 43.8 us -> 43.2 us  [shards(): pl.pallas_call(functools.partial(kernel, ORDER), out_shape=[pltpu.VMEM((2...]
where the time goes in v8:
time: 46.9 us; the launch traced here: 46.8 us
  Pallas kernels  45.3 us (97%)
  between operations  1.45 us (3%)
    pallas_call x1, Pallas kernels, shards(): pl.pallas_call(functools.partial(kernel, ORDER), out_shape=[pltpu.VMEM((2...  43.2 us
    pallas_call x1, Pallas kernels, shards(): pl.pallas_call(finish, out_shape=[jax.ShapeDtypeStruct((2048, 512), BF),...  2.11 us

profile of v8, /device:TPU:1, one launch (start us, length us, event | category | flops | bytes accessed | tf_op | source)
XLA Modules:
  0.0 46.8 jit_solution(8568527787154391426)
XLA Ops:
  1.3 43.2 %step.1 = (bf16[2048,512]{1,0:T(8,128)(2,1)S(1)}, bf16[2048,512]{1,0:T(8,128)(2,1)S(1)}, f32[2048,512]{1,0:T(8,128)S(1)}, bf16[512,512]{1,0:T(8,128)(2,1)S(1)}, ...) custom-call(bf16[440,512]{1,0:T(8,128)(2,1)} %bitcast.4, bf16[512,512]{1,0:T(8,128)(2,1)} %targ_hbm.1, ...), custom_call_target="tpu_custom_call" | custom-call | tf_op jit(solution)/shard_map/step/pallas_call | solution.py:293
  44.5 2.1 %finish.1 = (bf16[2048,512]{1,0:T(8,128)(2,1)}, f32[2,1024]{1,0:T(2,128)}) custom-call(bf16[2048,512]{1,0:T(8,128)(2,1)S(1)} %get-tuple-element.10.w_v, bf16[2048,512]{1,0:T(8,128)(2,1)S(1)} %get-tuple-element.11.ef_v, f32[2048,512]{1,0:T(8,128)S(1)} %get-tuple-element.12.g_v, bf16[512,512]{1,0:T(8,128)(2,1)S(1)} %get-tuple-element.13.rc_last, ...), custom_call_target="tpu_custom_call" | custom-call | tf_op jit(solution)/shard_map/finish/pallas_call | solution.py:341
